TPU v7x, 32 devices: a whole 2x2x4 slice. The times are simulated.
32 devices in a mesh: blk: 8 (over z, y), shard: 4 (over x, core).
Axes of the slice: x: 2, y: 2, z: 4, core: 2. Of those that a mesh axis runs over, the one named last changes fastest.
Arguments:
- weights: bfloat16 [8, 8192, 2048], P('blk', 'shard'), may hold values from -90 to 90
- warm_factor: float32 [8, 32, 2048], P('blk'), may hold values from -6 to 6
Outputs:
- new_weights: bfloat16 [8, 8192, 2048], P('blk', 'shard')
- new_factor: float32 [8, 32, 2048], P('blk', None, 'shard')
All inputs are finite; a program needn't handle non-finite values.
Results may differ from a plain program's by a relative error of at most 0.012.
Values may be sent and summed in bfloat16 or wider, within the bound.
No kernel may reach another device: no remote copies, remote signals or barrier semaphores. Data moves between devices by JAX's collectives and lax.ppermute only.
A program may use at most 64 MiB of HBM per device.

v0:
```python
import jax
import jax.numpy as jnp
from jax import lax
from jax.sharding import PartitionSpec as P

POWER = 4
MIXING = 1.0 / 3.0


def passed_along(value, axis, by):
    peers = lax.axis_size(axis)
    return lax.ppermute(value, axis, [(i, (i + by) % peers) for i in range(peers)])


def lower_solve(lower_factor, right_hand):
    return jax.scipy.linalg.solve_triangular(lower_factor, right_hand, lower=True)


def on_device(weights, warm_factor):
    local_weight = weights[0]
    own_factor = warm_factor[0]
    own_rounded = own_factor.astype(jnp.bfloat16)
    prior_rounded = passed_along(own_rounded, "blk", 1)
    rounded = jnp.stack([own_rounded, prior_rounded])
    width_piece = local_weight.shape[1] // lax.axis_size("shard")
    own_piece = jnp.stack([own_factor, own_factor])[:, :, :width_piece]
    left_rows = jnp.zeros((2, own_factor.shape[0], local_weight.shape[0]), jnp.bfloat16)
    for iteration in range(POWER):
        products = jnp.einsum(
            "ekc,rc->ekr", rounded, local_weight, preferred_element_type=jnp.float32
        )
        from_next = passed_along(products[1], "blk", -1)
        from_prior = passed_along(products[0], "blk", 1)
        raw_factor = jnp.stack([products[0] - from_next, from_prior - products[1]])
        gram = jnp.einsum("ekr,elr->ekl", raw_factor, raw_factor, precision=lax.Precision.HIGHEST)
        gram = lax.psum(gram, "shard")
        lower_factor = jnp.linalg.cholesky(gram)
        basis = jax.vmap(lower_solve)(lower_factor, raw_factor)
        left_rows = basis.astype(jnp.bfloat16)
        partials = jnp.einsum(
            "ekr,rc->ekc", left_rows, local_weight, preferred_element_type=jnp.float32
        )
        next_part = passed_along(partials[1], "blk", -1)
        prior_part = passed_along(partials[0], "blk", 1)
        factors = lax.psum(jnp.stack([partials[0] - next_part, prior_part - partials[1]]), "shard")
        own_piece = lax.dynamic_slice_in_dim(
            factors, lax.axis_index("shard") * width_piece, width_piece, 2
        )
        rounded = factors.astype(jnp.bfloat16)
    signed = jnp.concatenate([left_rows[1], -left_rows[0]], axis=0)
    factor_pair = jnp.concatenate([rounded[1], rounded[0]], axis=0)
    delta = jnp.einsum("jr,jc->rc", signed, factor_pair, preferred_element_type=jnp.float32)
    new_weight = (local_weight.astype(jnp.float32) + MIXING * delta).astype(jnp.bfloat16)
    return (new_weight[None], own_piece[0][None])


def solution(mesh):
    placed = (P("blk", "shard", None), P("blk", None, None))
    return jax.shard_map(
        on_device,
        mesh=mesh,
        in_specs=placed,
        out_specs=(P("blk", "shard", None), P("blk", None, "shard")),
        check_vma=False,
    )
```

profile of v0, /device:TPU:0, one launch (start us, length us, event | category | flops | bytes accessed | tf_op | source)
XLA Modules:
  0.0 363.7 jit_solution(13797275258302766750)
XLA Ops:
  7.2 1.0 convert_bitcast_fusion
  8.2 3.0 collective-permute-start
  11.2 1.0 convert_element_type.38
  12.2 5.6 %collective-permute-done = bf16[32,2048]{1,0:T(8,128)(2,1)S(1)} collective-permute-done((bf16[32,2048]{1,0:T(8,128)(2,1)S(1)}, bf16[32,2048]{1,0:T(8,128)(2,1)S(1)}, u32[]{:S(2)}, u32[]{:S(2)}) %collective-permute-start) | collective-permute-done | bytes 131104 | tf_op jit(solution)/shard_map/ppermute | solution.py:12
  17.7 6.0 %fusion.14 = f32[2,32,2048]{2,1,0:T(8,128)S(1)} fusion(bf16[1,2048,2048]{2,1,0:T(8,128)(2,1)} %param.5, bf16[1,32,2048]{2,1,0:T(8,128)(2,1)S(1)} %bitcast.173, bf16[1,32,2048]{2,1,0:T(8,128)(2,1)S(1)} %convert_element_type.38), kind=kOutput, calls=%fused_computation.15 | convolution fusion | flops 537001984 | bytes 9175040 | tf_op jit(solution)/shard_map/ekc,rc->ekr/dot_general | solution.py:29
  23.8 1.8 collective-permute-start.1
  25.6 0.3 collective-permute-start.2
  25.9 11.1 %collective-permute-done.1 = f32[32,2048]{1,0:T(8,128)S(1)} collective-permute-done((f32[32,2048]{1,0:T(8,128)S(1)}, f32[32,2048]{1,0:T(8,128)S(1)}, u32[]{:S(2)}, u32[]{:S(2)}) %collective-permute-start.1) | collective-permute-done | bytes 262176 | tf_op jit(solution)/shard_map/ppermute | solution.py:12
  37.0 0.6 fusion.20
  37.6 10.3 %psum.56 = f32[2,32,32]{1,2,0:T(8,128)S(1)} all-reduce(f32[2,32,32]{1,2,0:T(8,128)S(1)} %fusion.20), channel_id=1, replica_groups=mesh['blk'=8,'shard'=4] {'shard'}, use_global_device_ids=true, to_apply=%region_0.0 | all-reduce | flops 2048 | bytes 16384 | tf_op jit(solution)/shard_map/psum | solution.py:36
  48.0 5.9 %custom-call.12 = f32[2,32,32]{2,1,0:T(8,128)S(1)} custom-call(f32[2,32,32]{2,1,0:T(8,128)S(1)} %fusion.41), custom_call_target="Cholesky" | custom-call | tf_op jit(solution)/shard_map/jit(cholesky)/cholesky | solution.py:37
  53.9 0.1 compare_reduce_fusion.3
  54.1 4.9 %custom-call.13 = f32[2,1,32,32]{2,3,1,0:T(8,128)S(1)} custom-call(f32[2,1,32,32]{3,2,1,0:T(8,128)S(1)} %select_bitcast_fusion.3), custom_call_target="InvertDiagBlocksLowerTriangular" | custom-call | tf_op jit(solution)/shard_map/vmap(jit(_solve_triangular))/triangular_solve | solution.py:16
  59.0 0.7 convolution_convert_fusion.3
  59.6 5.0 %fusion.12 = f32[2,32,2048]{2,1,0:T(8,128)S(1)} fusion(bf16[2,32,2048]{2,1,0:T(8,128)(2,1)S(1)} %convolution_convert_fusion.3, bf16[1,2048,2048]{2,1,0:T(8,128)(2,1)} %param.5), kind=kOutput, calls=%fused_computation.13 | convolution fusion | flops 536870912 | bytes 9175040 | tf_op jit(solution)/shard_map/ekr,rc->ekc/dot_general | solution.py:40
  64.6 2.6 collective-permute-start.3
  67.2 11.4 %collective-permute-done.3 = f32[32,2048]{1,0:T(8,128)S(1)} collective-permute-done((f32[32,2048]{1,0:T(8,128)S(1)}, f32[32,2048]{1,0:T(8,128)S(1)}, u32[]{:S(2)}, u32[]{:S(2)}) %collective-permute-start.3) | collective-permute-done | bytes 262176 | tf_op jit(solution)/shard_map/ppermute | solution.py:12
  78.8 16.0 %all-reduce.6 = bf16[2,32,2048]{2,1,0:T(8,128)(2,1)S(1)} all-reduce(f32[2,32,2048]{2,1,0:T(8,128)S(1)} %pad_maximum_fusion.1), channel_id=1, replica_groups=mesh['blk'=8,'shard'=4] {'shard'}, use_global_device_ids=true, to_apply=%region_3.0 | all-reduce | flops 131072 | bytes 786432 | tf_op jit(solution)/shard_map/psum | solution.py:45
  94.7 6.0 %fusion.10 = f32[2,32,2048]{2,1,0:T(8,128)S(1)} fusion(bf16[1,2048,2048]{2,1,0:T(8,128)(2,1)} %param.5, bf16[2,32,2048]{2,1,0:T(8,128)(2,1)S(1)} %all-reduce.6), kind=kOutput, calls=%fused_computation.11 | convolution fusion | flops 536870912 | bytes 9175040 | tf_op jit(solution)/shard_map/ekc,rc->ekr/dot_general | solution.py:29
  100.8 2.7 collective-permute-start.5
  103.6 5.8 %collective-permute-done.5 = f32[32,2048]{1,0:T(8,128)S(1)} collective-permute-done((f32[32,2048]{1,0:T(8,128)S(1)}, f32[32,2048]{1,0:T(8,128)S(1)}, u32[]{:S(2)}, u32[]{:S(2)}) %collective-permute-start.5) | collective-permute-done | bytes 262176 | tf_op jit(solution)/shard_map/ppermute | solution.py:12
  109.4 4.9 %collective-permute-done.6 = f32[32,2048]{1,0:T(8,128)S(1)} collective-permute-done((f32[32,2048]{1,0:T(8,128)S(1)}, f32[32,2048]{1,0:T(8,128)S(1)}, u32[]{:S(2)}, u32[]{:S(2)}) %collective-permute-start.6) | collective-permute-done | bytes 262176 | tf_op jit(solution)/shard_map/ppermute | solution.py:12
  114.4 0.6 fusion.19
  114.9 10.3 %psum.58 = f32[2,32,32]{1,2,0:T(8,128)S(1)} all-reduce(f32[2,32,32]{1,2,0:T(8,128)S(1)} %fusion.19), channel_id=1, replica_groups=mesh['blk'=8,'shard'=4] {'shard'}, use_global_device_ids=true, to_apply=%region_4.0 | all-reduce | flops 2048 | bytes 16384 | tf_op jit(solution)/shard_map/psum | solution.py:36
  125.3 5.9 %custom-call.14 = f32[2,32,32]{2,1,0:T(8,128)S(1)} custom-call(f32[2,32,32]{2,1,0:T(8,128)S(1)} %fusion.39), custom_call_target="Cholesky" | custom-call | tf_op jit(solution)/shard_map/jit(cholesky)/cholesky | solution.py:37
  131.2 0.1 compare_reduce_fusion.2
  131.4 4.9 %custom-call.15 = f32[2,1,32,32]{2,3,1,0:T(8,128)S(1)} custom-call(f32[2,1,32,32]{3,2,1,0:T(8,128)S(1)} %select_bitcast_fusion.2), custom_call_target="InvertDiagBlocksLowerTriangular" | custom-call | tf_op jit(solution)/shard_map/vmap(jit(_solve_triangular))/triangular_solve | solution.py:16
  136.3 0.7 convolution_convert_fusion.2
  136.9 5.0 %fusion.8 = f32[2,32,2048]{2,1,0:T(8,128)S(1)} fusion(bf16[2,32,2048]{2,1,0:T(8,128)(2,1)S(1)} %convolution_convert_fusion.2, bf16[1,2048,2048]{2,1,0:T(8,128)(2,1)} %param.5), kind=kOutput, calls=%fused_computation.9 | convolution fusion | flops 536870912 | bytes 9175040 | tf_op jit(solution)/shard_map/ekr,rc->ekc/dot_general | solution.py:40
  142.0 3.5 collective-permute-start.7
  145.5 10.6 %collective-permute-done.7 = f32[32,2048]{1,0:T(8,128)S(1)} collective-permute-done((f32[32,2048]{1,0:T(8,128)S(1)}, f32[32,2048]{1,0:T(8,128)S(1)}, u32[]{:S(2)}, u32[]{:S(2)}) %collective-permute-start.7) | collective-permute-done | bytes 262176 | tf_op jit(solution)/shard_map/ppermute | solution.py:12
  156.0 0.2 collective-permute-done.8
  156.3 16.8 %all-reduce.7 = bf16[2,32,2048]{2,1,0:T(8,128)(2,1)S(1)} all-reduce(f32[2,32,2048]{2,1,0:T(8,128)S(1)} %pad_maximum_fusion.3), channel_id=1, replica_groups=mesh['blk'=8,'shard'=4] {'shard'}, use_global_device_ids=true, to_apply=%region_5.0 | all-reduce | flops 131072 | bytes 786432 | tf_op jit(solution)/shard_map/psum | solution.py:45
  173.1 6.0 %fusion.6 = f32[2,32,2048]{2,1,0:T(8,128)S(1)} fusion(bf16[1,2048,2048]{2,1,0:T(8,128)(2,1)} %param.5, bf16[2,32,2048]{2,1,0:T(8,128)(2,1)S(1)} %all-reduce.7), kind=kOutput, calls=%fused_computation.7 | convolution fusion | flops 536870912 | bytes 9175040 | tf_op jit(solution)/shard_map/ekc,rc->ekr/dot_general | solution.py:29
  179.2 2.5 collective-permute-start.9
  181.8 11.8 %collective-permute-done.9 = f32[32,2048]{1,0:T(8,128)S(1)} collective-permute-done((f32[32,2048]{1,0:T(8,128)S(1)}, f32[32,2048]{1,0:T(8,128)S(1)}, u32[]{:S(2)}, u32[]{:S(2)}) %collective-permute-start.9) | collective-permute-done | bytes 262176 | tf_op jit(solution)/shard_map/ppermute | solution.py:12
  193.6 0.6 fusion.18
  194.2 10.5 %psum.60 = f32[2,32,32]{1,2,0:T(8,128)S(1)} all-reduce(f32[2,32,32]{1,2,0:T(8,128)S(1)} %fusion.18), channel_id=1, replica_groups=mesh['blk'=8,'shard'=4] {'shard'}, use_global_device_ids=true, to_apply=%region_6.0 | all-reduce | flops 2048 | bytes 16384 | tf_op jit(solution)/shard_map/psum | solution.py:36
  204.8 5.9 %custom-call.16 = f32[2,32,32]{2,1,0:T(8,128)S(1)} custom-call(f32[2,32,32]{2,1,0:T(8,128)S(1)} %fusion.37), custom_call_target="Cholesky" | custom-call | tf_op jit(solution)/shard_map/jit(cholesky)/cholesky | solution.py:37
  210.7 0.1 compare_reduce_fusion.1
  210.9 4.9 %custom-call.17 = f32[2,1,32,32]{2,3,1,0:T(8,128)S(1)} custom-call(f32[2,1,32,32]{3,2,1,0:T(8,128)S(1)} %select_bitcast_fusion.1), custom_call_target="InvertDiagBlocksLowerTriangular" | custom-call | tf_op jit(solution)/shard_map/vmap(jit(_solve_triangular))/triangular_solve | solution.py:16
  215.8 0.7 convolution_convert_fusion.1
  216.5 5.0 %fusion.4 = f32[2,32,2048]{2,1,0:T(8,128)S(1)} fusion(bf16[2,32,2048]{2,1,0:T(8,128)(2,1)S(1)} %convolution_convert_fusion.1, bf16[1,2048,2048]{2,1,0:T(8,128)(2,1)} %param.5), kind=kOutput, calls=%fused_computation.5 | convolution fusion | flops 536870912 | bytes 9175040 | tf_op jit(solution)/shard_map/ekr,rc->ekc/dot_general | solution.py:40
  221.5 1.7 collective-permute-start.11
  223.2 0.4 collective-permute-start.12
  223.6 11.3 %collective-permute-done.11 = f32[32,2048]{1,0:T(8,128)S(1)} collective-permute-done((f32[32,2048]{1,0:T(8,128)S(1)}, f32[32,2048]{1,0:T(8,128)S(1)}, u32[]{:S(2)}, u32[]{:S(2)}) %collective-permute-start.11) | collective-permute-done | bytes 262176 | tf_op jit(solution)/shard_map/ppermute | solution.py:12
  235.0 15.9 %all-reduce.8 = bf16[2,32,2048]{2,1,0:T(8,128)(2,1)S(1)} all-reduce(f32[2,32,2048]{2,1,0:T(8,128)S(1)} %pad_maximum_fusion.5), channel_id=1, replica_groups=mesh['blk'=8,'shard'=4] {'shard'}, use_global_device_ids=true, to_apply=%region_7.0 | all-reduce | flops 131072 | bytes 786432 | tf_op jit(solution)/shard_map/psum | solution.py:45
  250.9 6.0 %fusion.2 = f32[2,32,2048]{2,1,0:T(8,128)S(1)} fusion(bf16[1,2048,2048]{2,1,0:T(8,128)(2,1)} %param.5, bf16[2,32,2048]{2,1,0:T(8,128)(2,1)S(1)} %all-reduce.8), kind=kOutput, calls=%fused_computation.3 | convolution fusion | flops 536870912 | bytes 9175040 | tf_op jit(solution)/shard_map/ekc,rc->ekr/dot_general | solution.py:29
  257.0 3.0 collective-permute-start.13
  260.0 11.2 %collective-permute-done.13 = f32[32,2048]{1,0:T(8,128)S(1)} collective-permute-done((f32[32,2048]{1,0:T(8,128)S(1)}, f32[32,2048]{1,0:T(8,128)S(1)}, u32[]{:S(2)}, u32[]{:S(2)}) %collective-permute-start.13) | collective-permute-done | bytes 262176 | tf_op jit(solution)/shard_map/ppermute | solution.py:12
  271.3 0.6 fusion.17
  271.8 10.8 %psum.62 = f32[2,32,32]{1,2,0:T(8,128)S(1)} all-reduce(f32[2,32,32]{1,2,0:T(8,128)S(1)} %fusion.17), channel_id=1, replica_groups=mesh['blk'=8,'shard'=4] {'shard'}, use_global_device_ids=true, to_apply=%region_8.11 | all-reduce | flops 2048 | bytes 16384 | tf_op jit(solution)/shard_map/psum | solution.py:36
  282.7 5.9 %custom-call.18 = f32[2,32,32]{2,1,0:T(8,128)S(1)} custom-call(f32[2,32,32]{2,1,0:T(8,128)S(1)} %fusion.35), custom_call_target="Cholesky" | custom-call | tf_op jit(solution)/shard_map/jit(cholesky)/cholesky | solution.py:37
  288.8 4.9 %custom-call.19 = f32[2,1,32,32]{2,3,1,0:T(8,128)S(1)} custom-call(f32[2,1,32,32]{3,2,1,0:T(8,128)S(1)} %select_bitcast_fusion), custom_call_target="InvertDiagBlocksLowerTriangular" | custom-call | tf_op jit(solution)/shard_map/vmap(jit(_solve_triangular))/triangular_solve | solution.py:16
  293.8 0.6 convolution_convert_fusion
  294.4 4.9 %fusion = f32[2,32,2048]{2,1,0:T(8,128)S(1)} fusion(bf16[2,32,2048]{2,1,0:T(8,128)(2,1)S(1)} %convolution_convert_fusion, bf16[1,2048,2048]{2,1,0:T(8,128)(2,1)} %param.5), kind=kOutput, calls=%fused_computation.1 | convolution fusion | flops 536870912 | bytes 9175040 | tf_op jit(solution)/shard_map/ekr,rc->ekc/dot_general | solution.py:40
  299.4 3.5 collective-permute-start.15
  302.9 10.7 %collective-permute-done.15 = f32[32,2048]{1,0:T(8,128)S(1)} collective-permute-done((f32[32,2048]{1,0:T(8,128)S(1)}, f32[32,2048]{1,0:T(8,128)S(1)}, u32[]{:S(2)}, u32[]{:S(2)}) %collective-permute-start.15) | collective-permute-done | bytes 262176 | tf_op jit(solution)/shard_map/ppermute | solution.py:12
  313.5 0.2 collective-permute-done.16
  313.8 0.8 pad_maximum_fusion.7
  314.6 32.8 %all-reduce.5.cloned.1.call-done = f32[2,32,2048]{2,1,0:T(8,128)} async-done(((f32[2,32,2048]{2,1,0:T(8,128)}), f32[2,32,2048]{2,1,0:T(8,128)}) %all-reduce.5.cloned.1.call-update) | async-done | bytes 524304 | tf_op jit(solution)/shard_map/psum | solution.py:45
  347.4 1.1 convert_element_type.47
  348.5 6.9 %fusion.16 = bf16[1,2048,2048]{2,1,0:T(8,128)(2,1)} fusion(bf16[1,2048,2048]{2,1,0:T(8,128)(2,1)} %param.5, bf16[32,2048]{1,0:T(8,128)(2,1)S(1)} %get-tuple-element.39, bf16[32,2048]{1,0:T(8,128)(2,1)S(1)} %get-tuple-element.38, bf16[32,2048]{1,0:T(8,128)(2,1)S(1)} %get-tuple-element.37, bf16[32,2048]{1,0:T(8,128)(2,1)S(1)} %get-tuple-element.36), kind=kOutput, calls=%fused_computation.17 | convolution fusion | flops 554696704 | bytes 17301504 | tf_op jit(solution)/shard_map/jr,jc->rc/dot_general | solution.py:52
  355.4 1.5 constant_dynamic-slice_fusion
  (53 shorter events, 2.0 us)
Async XLA Ops:
  7.2 340.2 %all-reduce.5.cloned.1.call-start = ((), (), s32[]{:S(2)}) async-start(), calls=%async_computation | async-start | bytes 1048576 | tf_op jit(solution)/shard_map/psum | solution.py:45
  8.2 9.6 %collective-permute-start = (bf16[32,2048]{1,0:T(8,128)(2,1)S(1)}, bf16[32,2048]{1,0:T(8,128)(2,1)S(1)}, u32[]{:S(2)}, u32[]{:S(2)}) collective-permute-start(bf16[32,2048]{1,0:T(8,128)(2,1)S(1)} %convert_bitcast_fusion), channel_id=1, source_target_pairs={{0,4},{4,8},{8,12},{12,16},{16,20},{20,24},{24,28},{28,0},{1,5},{5... | collective-permute-start | bytes 393224 | tf_op jit(solution)/shard_map/ppermute | solution.py:12
  23.8 13.2 %collective-permute-start.1 = (f32[32,2048]{1,0:T(8,128)S(1)}, f32[32,2048]{1,0:T(8,128)S(1)}, u32[]{:S(2)}, u32[]{:S(2)}) collective-permute-start(f32[32,2048]{1,0:T(8,128)S(1)} %get-tuple-element.34), channel_id=1, source_target_pairs={{0,28},{4,0},{8,4},{12,8},{16,12},{20,16},{24,20},{28,24},{1,29},{... | collective-permute-start | bytes 786440 | tf_op jit(solution)/shard_map/ppermute | solution.py:12
  25.6 11.4 %collective-permute-start.2 = (f32[32,2048]{1,0:T(8,128)S(1)}, f32[32,2048]{1,0:T(8,128)S(1)}, u32[]{:S(2)}, u32[]{:S(2)}) collective-permute-start(f32[32,2048]{1,0:T(8,128)S(1)} %get-tuple-element.35), channel_id=1, source_target_pairs={{0,4},{4,8},{8,12},{12,16},{16,20},{20,24},{24,28},{28,0},{1,5},{5... | collective-permute-start | bytes 786440 | tf_op jit(solution)/shard_map/ppermute | solution.py:12
  64.6 14.0 %collective-permute-start.3 = (f32[32,2048]{1,0:T(8,128)S(1)}, f32[32,2048]{1,0:T(8,128)S(1)}, u32[]{:S(2)}, u32[]{:S(2)}) collective-permute-start(f32[32,2048]{1,0:T(8,128)S(1)} %get-tuple-element.30), channel_id=1, source_target_pairs={{0,28},{4,0},{8,4},{12,8},{16,12},{20,16},{24,20},{28,24},{1,29},{... | collective-permute-start | bytes 786440 | tf_op jit(solution)/shard_map/ppermute | solution.py:12
  67.2 11.4 %collective-permute-start.4 = (f32[32,2048]{1,0:T(8,128)S(1)}, f32[32,2048]{1,0:T(8,128)S(1)}, u32[]{:S(2)}, u32[]{:S(2)}) collective-permute-start(f32[32,2048]{1,0:T(8,128)S(1)} %get-tuple-element.31), channel_id=1, source_target_pairs={{0,4},{4,8},{8,12},{12,16},{16,20},{20,24},{24,28},{28,0},{1,5},{5... | collective-permute-start | bytes 786440 | tf_op jit(solution)/shard_map/ppermute | solution.py:12
  100.8 8.6 %collective-permute-start.5 = (f32[32,2048]{1,0:T(8,128)S(1)}, f32[32,2048]{1,0:T(8,128)S(1)}, u32[]{:S(2)}, u32[]{:S(2)}) collective-permute-start(f32[32,2048]{1,0:T(8,128)S(1)} %get-tuple-element.26), channel_id=1, source_target_pairs={{0,28},{4,0},{8,4},{12,8},{16,12},{20,16},{24,20},{28,24},{1,29},{... | collective-permute-start | bytes 786440 | tf_op jit(solution)/shard_map/ppermute | solution.py:12
  103.6 10.7 %collective-permute-start.6 = (f32[32,2048]{1,0:T(8,128)S(1)}, f32[32,2048]{1,0:T(8,128)S(1)}, u32[]{:S(2)}, u32[]{:S(2)}) collective-permute-start(f32[32,2048]{1,0:T(8,128)S(1)} %get-tuple-element.27), channel_id=1, source_target_pairs={{0,4},{4,8},{8,12},{12,16},{16,20},{20,24},{24,28},{28,0},{1,5},{5... | collective-permute-start | bytes 786440 | tf_op jit(solution)/shard_map/ppermute | solution.py:12
  142.0 14.1 %collective-permute-start.7 = (f32[32,2048]{1,0:T(8,128)S(1)}, f32[32,2048]{1,0:T(8,128)S(1)}, u32[]{:S(2)}, u32[]{:S(2)}) collective-permute-start(f32[32,2048]{1,0:T(8,128)S(1)} %get-tuple-element.22), channel_id=1, source_target_pairs={{0,28},{4,0},{8,4},{12,8},{16,12},{20,16},{24,20},{28,24},{1,29},{... | collective-permute-start | bytes 786440 | tf_op jit(solution)/shard_map/ppermute | solution.py:12
  145.5 10.7 %collective-permute-start.8 = (f32[32,2048]{1,0:T(8,128)S(1)}, f32[32,2048]{1,0:T(8,128)S(1)}, u32[]{:S(2)}, u32[]{:S(2)}) collective-permute-start(f32[32,2048]{1,0:T(8,128)S(1)} %get-tuple-element.23), channel_id=1, source_target_pairs={{0,4},{4,8},{8,12},{12,16},{16,20},{20,24},{24,28},{28,0},{1,5},{5... | collective-permute-start | bytes 786440 | tf_op jit(solution)/shard_map/ppermute | solution.py:12
  179.2 14.4 %collective-permute-start.9 = (f32[32,2048]{1,0:T(8,128)S(1)}, f32[32,2048]{1,0:T(8,128)S(1)}, u32[]{:S(2)}, u32[]{:S(2)}) collective-permute-start(f32[32,2048]{1,0:T(8,128)S(1)} %get-tuple-element.18), channel_id=1, source_target_pairs={{0,28},{4,0},{8,4},{12,8},{16,12},{20,16},{24,20},{28,24},{1,29},{... | collective-permute-start | bytes 786440 | tf_op jit(solution)/shard_map/ppermute | solution.py:12
  181.7 11.9 %collective-permute-start.10 = (f32[32,2048]{1,0:T(8,128)S(1)}, f32[32,2048]{1,0:T(8,128)S(1)}, u32[]{:S(2)}, u32[]{:S(2)}) collective-permute-start(f32[32,2048]{1,0:T(8,128)S(1)} %get-tuple-element.19), channel_id=1, source_target_pairs={{0,4},{4,8},{8,12},{12,16},{16,20},{20,24},{24,28},{28,0},{1,5},{5... | collective-permute-start | bytes 786440 | tf_op jit(solution)/shard_map/ppermute | solution.py:12
  221.5 13.4 %collective-permute-start.11 = (f32[32,2048]{1,0:T(8,128)S(1)}, f32[32,2048]{1,0:T(8,128)S(1)}, u32[]{:S(2)}, u32[]{:S(2)}) collective-permute-start(f32[32,2048]{1,0:T(8,128)S(1)} %get-tuple-element.14), channel_id=1, source_target_pairs={{0,28},{4,0},{8,4},{12,8},{16,12},{20,16},{24,20},{28,24},{1,29},{... | collective-permute-start | bytes 786440 | tf_op jit(solution)/shard_map/ppermute | solution.py:12
  223.2 11.7 %collective-permute-start.12 = (f32[32,2048]{1,0:T(8,128)S(1)}, f32[32,2048]{1,0:T(8,128)S(1)}, u32[]{:S(2)}, u32[]{:S(2)}) collective-permute-start(f32[32,2048]{1,0:T(8,128)S(1)} %get-tuple-element.15), channel_id=1, source_target_pairs={{0,4},{4,8},{8,12},{12,16},{16,20},{20,24},{24,28},{28,0},{1,5},{5... | collective-permute-start | bytes 786440 | tf_op jit(solution)/shard_map/ppermute | solution.py:12
  257.0 14.2 %collective-permute-start.13 = (f32[32,2048]{1,0:T(8,128)S(1)}, f32[32,2048]{1,0:T(8,128)S(1)}, u32[]{:S(2)}, u32[]{:S(2)}) collective-permute-start(f32[32,2048]{1,0:T(8,128)S(1)} %get-tuple-element.10), channel_id=1, source_target_pairs={{0,28},{4,0},{8,4},{12,8},{16,12},{20,16},{24,20},{28,24},{1,29},{... | collective-permute-start | bytes 786440 | tf_op jit(solution)/shard_map/ppermute | solution.py:12
  260.0 11.2 %collective-permute-start.14 = (f32[32,2048]{1,0:T(8,128)S(1)}, f32[32,2048]{1,0:T(8,128)S(1)}, u32[]{:S(2)}, u32[]{:S(2)}) collective-permute-start(f32[32,2048]{1,0:T(8,128)S(1)} %get-tuple-element.11), channel_id=1, source_target_pairs={{0,4},{4,8},{8,12},{12,16},{16,20},{20,24},{24,28},{28,0},{1,5},{5... | collective-permute-start | bytes 786440 | tf_op jit(solution)/shard_map/ppermute | solution.py:12
  299.4 14.1 %collective-permute-start.15 = (f32[32,2048]{1,0:T(8,128)S(1)}, f32[32,2048]{1,0:T(8,128)S(1)}, u32[]{:S(2)}, u32[]{:S(2)}) collective-permute-start(f32[32,2048]{1,0:T(8,128)S(1)} %get-tuple-element.6), channel_id=1, source_target_pairs={{0,28},{4,0},{8,4},{12,8},{16,12},{20,16},{24,20},{28,24},{1,29},{... | collective-permute-start | bytes 786440 | tf_op jit(solution)/shard_map/ppermute | solution.py:12
  302.9 10.8 %collective-permute-start.16 = (f32[32,2048]{1,0:T(8,128)S(1)}, f32[32,2048]{1,0:T(8,128)S(1)}, u32[]{:S(2)}, u32[]{:S(2)}) collective-permute-start(f32[32,2048]{1,0:T(8,128)S(1)} %get-tuple-element.7), channel_id=1, source_target_pairs={{0,4},{4,8},{8,12},{12,16},{16,20},{20,24},{24,28},{28,0},{1,5},{5... | collective-permute-start | bytes 786440 | tf_op jit(solution)/shard_map/ppermute | solution.py:12
Sparse Core Ops, SparseCore 0:
  314.7 32.6 all-reduce.4
where the time goes:
time: 364 us
  waiting for transfers between devices  127 us (35%)
  blocking collectives  90.5 us (25%)
  matrix products  55.7 us (15%)
  other arithmetic  48.5 us (13%)
  starting transfers between devices  25.1 us (7%)
  between operations  14.3 us (4%)
    ppermute x17, waiting for transfers between devices, passed_along(): lax.ppermute(value, axis, [(i, (i + by) % peers) for i in range(peers)])  94.6 us
    psum x3, blocking collectives, on_device(): lax.psum(jnp.stack([partials[0] - next_part, prior_part - partials[1]]),...  48.7 us
    psum x4, blocking collectives, on_device(): gram = lax.psum(gram, 'shard')  41.9 us
    psum x1, waiting for transfers between devices, on_device(): lax.psum(jnp.stack([partials[0] - next_part, prior_part - partials[1]]),...  32.8 us
    ppermute x17, starting transfers between devices, passed_along(): lax.ppermute(value, axis, [(i, (i + by) % peers) for i in range(peers)])  25.1 us
    dot_general x4, matrix products, on_device(): jnp.einsum('ekc,rc->ekr', rounded, local_weight, preferred_element_type=j...  24.1 us
    another operation x13, other arithmetic, on_device(): lower_factor = jnp.linalg.cholesky(gram)  24.1 us
    another operation x9, other arithmetic, lower_solve(): jax.scipy.linalg.solve_triangular(lower_factor, right_hand, lower=True)  20 us
  transfers between devices with their start and end apart: 18, of which 13 were waited for; matrix products, arithmetic and copies ran while one was open for 0% of the time, Pallas kernels for 0%

commit v1 on v0

--- a/solution.py
+++ b/solution.py
@@ -33,7 +33,15 @@
         from_prior = passed_along(products[0], "blk", 1)
         raw_factor = jnp.stack([products[0] - from_next, from_prior - products[1]])
         gram = jnp.einsum("ekr,elr->ekl", raw_factor, raw_factor, precision=lax.Precision.HIGHEST)
-        gram = lax.psum(gram, "shard")
+
+        def local_data_use(v0, device_axis):
+            num = jax.lax.axis_size(device_axis)
+            aux = v0
+            for nth in [[(c, c ^ p) for c in range(num)] for p in (1, 2, 4, 8, 16) if p < num]:
+                aux = aux + jax.lax.ppermute(aux, axis_name=device_axis, perm=nth)
+            return aux
+
+        gram = local_data_use(gram, "shard")
         lower_factor = jnp.linalg.cholesky(gram)
         basis = jax.vmap(lower_solve)(lower_factor, raw_factor)
         left_rows = basis.astype(jnp.bfloat16)

time: 364 us -> 341 us (0.937)
  blocking collectives: 90.5 us -> 48.6 us
  waiting for transfers between devices: 127 us -> 144 us
    psum x4 -> x0, blocking collectives: 41.9 us -> none  [on_device(): gram = lax.psum(gram, 'shard')]
    ppermute x0 -> x8, waiting for transfers between devices: none -> 17.6 us  [local_data_use(): aux = aux + jax.lax.ppermute(aux, axis_name=device_axis, perm=nth)]
  transfers between devices with their start and end apart: 18 -> 26, of which waited for: 13 -> 19; matrix products, arithmetic and copies ran while one was open for 0% -> 0% of each run, Pallas kernels for 0% -> 0%
where the time goes in v1:
time: 341 us; the launch traced here: 340 us
  waiting for transfers between devices  144 us (42%)
  matrix products  55.7 us (16%)
  other arithmetic  48.6 us (14%)
  blocking collectives  48.6 us (14%)
  starting transfers between devices  27.4 us (8%)
  between operations  14.3 us (4%)
    ppermute x17, waiting for transfers between devices, passed_along(): lax.ppermute(value, axis, [(i, (i + by) % peers) for i in range(peers)])  92.8 us
    psum x3, blocking collectives, on_device(): lax.psum(jnp.stack([partials[0] - next_part, prior_part - partials[1]]),...  48.6 us
    psum x1, waiting for transfers between devices, on_device(): lax.psum(jnp.stack([partials[0] - next_part, prior_part - partials[1]]),...  33.4 us
    ppermute x17, starting transfers between devices, passed_along(): lax.ppermute(value, axis, [(i, (i + by) % peers) for i in range(peers)])  24.3 us
    dot_general x4, matrix products, on_device(): jnp.einsum('ekc,rc->ekr', rounded, local_weight, preferred_element_type=j...  24.1 us
    another operation x13, other arithmetic, on_device(): lower_factor = jnp.linalg.cholesky(gram)  24.1 us
    another operation x9, other arithmetic, lower_solve(): jax.scipy.linalg.solve_triangular(lower_factor, right_hand, lower=True)  20 us
    dot_general x4, matrix products, on_device(): jnp.einsum('ekr,rc->ekc', left_rows, local_weight, preferred_element_type...  19.8 us
  transfers between devices with their start and end apart: 26, of which 19 were waited for; matrix products, arithmetic and copies ran while one was open for 0% of the time, Pallas kernels for 0%

profile of v1, /device:TPU:0, one launch (start us, length us, event | category | flops | bytes accessed | tf_op | source)
XLA Modules:
  0.0 340.4 jit_solution(17551521771553519867)
XLA Ops:
  7.2 1.0 convert_bitcast_fusion
  8.2 3.0 collective-permute-start
  11.2 1.0 convert_element_type.38
  12.2 5.6 %collective-permute-done = bf16[32,2048]{1,0:T(8,128)(2,1)S(1)} collective-permute-done((bf16[32,2048]{1,0:T(8,128)(2,1)S(1)}, bf16[32,2048]{1,0:T(8,128)(2,1)S(1)}, u32[]{:S(2)}, u32[]{:S(2)}) %collective-permute-start) | collective-permute-done | bytes 131104 | tf_op jit(solution)/shard_map/ppermute | solution.py:12
  17.7 6.0 %fusion.14 = f32[2,32,2048]{2,1,0:T(8,128)S(1)} fusion(bf16[1,2048,2048]{2,1,0:T(8,128)(2,1)} %param.5, bf16[1,32,2048]{2,1,0:T(8,128)(2,1)S(1)} %bitcast.173, bf16[1,32,2048]{2,1,0:T(8,128)(2,1)S(1)} %convert_element_type.38), kind=kOutput, calls=%fused_computation.15 | convolution fusion | flops 537001984 | bytes 9175040 | tf_op jit(solution)/shard_map/ekc,rc->ekr/dot_general | solution.py:29
  23.8 1.8 collective-permute-start.1
  25.9 11.1 %collective-permute-done.1 = f32[32,2048]{1,0:T(8,128)S(1)} collective-permute-done((f32[32,2048]{1,0:T(8,128)S(1)}, f32[32,2048]{1,0:T(8,128)S(1)}, u32[]{:S(2)}, u32[]{:S(2)}) %collective-permute-start.1) | collective-permute-done | bytes 262176 | tf_op jit(solution)/shard_map/ppermute | solution.py:12
  37.0 0.6 fusion.20
  37.7 1.2 collective-permute-done.3
  38.9 1.3 collective-permute-start.4
  40.2 2.6 collective-permute-done.4
  42.9 5.9 %custom-call.12 = f32[2,32,32]{2,1,0:T(8,128)S(1)} custom-call(f32[2,32,32]{2,1,0:T(8,128)S(1)} %fusion.41), custom_call_target="Cholesky" | custom-call | tf_op jit(solution)/shard_map/jit(cholesky)/cholesky | solution.py:45
  49.0 4.9 %custom-call.13 = f32[2,1,32,32]{2,3,1,0:T(8,128)S(1)} custom-call(f32[2,1,32,32]{3,2,1,0:T(8,128)S(1)} %select_bitcast_fusion.3), custom_call_target="InvertDiagBlocksLowerTriangular" | custom-call | tf_op jit(solution)/shard_map/vmap(jit(_solve_triangular))/triangular_solve | solution.py:16
  53.9 0.7 convolution_convert_fusion.3
  54.6 5.0 %fusion.12 = f32[2,32,2048]{2,1,0:T(8,128)S(1)} fusion(bf16[2,32,2048]{2,1,0:T(8,128)(2,1)S(1)} %convolution_convert_fusion.3, bf16[1,2048,2048]{2,1,0:T(8,128)(2,1)} %param.5), kind=kOutput, calls=%fused_computation.13 | convolution fusion | flops 536870912 | bytes 9175040 | tf_op jit(solution)/shard_map/ekr,rc->ekc/dot_general | solution.py:48
  59.6 2.6 collective-permute-start.5
  62.2 10.3 %collective-permute-done.5 = f32[32,2048]{1,0:T(8,128)S(1)} collective-permute-done((f32[32,2048]{1,0:T(8,128)S(1)}, f32[32,2048]{1,0:T(8,128)S(1)}, u32[]{:S(2)}, u32[]{:S(2)}) %collective-permute-start.5) | collective-permute-done | bytes 262176 | tf_op jit(solution)/shard_map/ppermute | solution.py:12
  72.6 16.2 %all-reduce.6 = bf16[2,32,2048]{2,1,0:T(8,128)(2,1)S(1)} all-reduce(f32[2,32,2048]{2,1,0:T(8,128)S(1)} %pad_maximum_fusion.1), channel_id=1, replica_groups=mesh['blk'=8,'shard'=4] {'shard'}, use_global_device_ids=true, to_apply=%region_2.0 | all-reduce | flops 131072 | bytes 786432 | tf_op jit(solution)/shard_map/psum | solution.py:53
  88.8 6.0 %fusion.10 = f32[2,32,2048]{2,1,0:T(8,128)S(1)} fusion(bf16[1,2048,2048]{2,1,0:T(8,128)(2,1)} %param.5, bf16[2,32,2048]{2,1,0:T(8,128)(2,1)S(1)} %all-reduce.6), kind=kOutput, calls=%fused_computation.11 | convolution fusion | flops 536870912 | bytes 9175040 | tf_op jit(solution)/shard_map/ekc,rc->ekr/dot_general | solution.py:29
  94.9 2.8 collective-permute-start.7
  97.7 11.2 %collective-permute-done.7 = f32[32,2048]{1,0:T(8,128)S(1)} collective-permute-done((f32[32,2048]{1,0:T(8,128)S(1)}, f32[32,2048]{1,0:T(8,128)S(1)}, u32[]{:S(2)}, u32[]{:S(2)}) %collective-permute-start.7) | collective-permute-done | bytes 262176 | tf_op jit(solution)/shard_map/ppermute | solution.py:12
  109.0 0.6 fusion.19
  109.6 1.2 collective-permute-done.9
  110.9 3.8 %collective-permute-done.10 = f32[2,32,32]{1,2,0:T(8,128)S(1)} collective-permute-done((f32[2,32,32]{1,2,0:T(8,128)S(1)}, f32[2,32,32]{1,2,0:T(8,128)S(1)}, u32[]{:S(2)}, u32[]{:S(2)}) %collective-permute-start.10) | collective-permute-done | bytes 8224 | tf_op jit(solution)/shard_map/ppermute | solution.py:41
  114.8 5.9 %custom-call.14 = f32[2,32,32]{2,1,0:T(8,128)S(1)} custom-call(f32[2,32,32]{2,1,0:T(8,128)S(1)} %fusion.39), custom_call_target="Cholesky" | custom-call | tf_op jit(solution)/shard_map/jit(cholesky)/cholesky | solution.py:45
  120.9 4.9 %custom-call.15 = f32[2,1,32,32]{2,3,1,0:T(8,128)S(1)} custom-call(f32[2,1,32,32]{3,2,1,0:T(8,128)S(1)} %select_bitcast_fusion.2), custom_call_target="InvertDiagBlocksLowerTriangular" | custom-call | tf_op jit(solution)/shard_map/vmap(jit(_solve_triangular))/triangular_solve | solution.py:16
  125.8 0.7 convolution_convert_fusion.2
  126.5 5.0 %fusion.8 = f32[2,32,2048]{2,1,0:T(8,128)S(1)} fusion(bf16[2,32,2048]{2,1,0:T(8,128)(2,1)S(1)} %convolution_convert_fusion.2, bf16[1,2048,2048]{2,1,0:T(8,128)(2,1)} %param.5), kind=kOutput, calls=%fused_computation.9 | convolution fusion | flops 536870912 | bytes 9175040 | tf_op jit(solution)/shard_map/ekr,rc->ekc/dot_general | solution.py:48
  131.5 2.8 collective-permute-start.11
  134.3 10.1 %collective-permute-done.11 = f32[32,2048]{1,0:T(8,128)S(1)} collective-permute-done((f32[32,2048]{1,0:T(8,128)S(1)}, f32[32,2048]{1,0:T(8,128)S(1)}, u32[]{:S(2)}, u32[]{:S(2)}) %collective-permute-start.11) | collective-permute-done | bytes 262176 | tf_op jit(solution)/shard_map/ppermute | solution.py:12
  144.5 16.4 %all-reduce.7 = bf16[2,32,2048]{2,1,0:T(8,128)(2,1)S(1)} all-reduce(f32[2,32,2048]{2,1,0:T(8,128)S(1)} %pad_maximum_fusion.3), channel_id=1, replica_groups=mesh['blk'=8,'shard'=4] {'shard'}, use_global_device_ids=true, to_apply=%region_3.0 | all-reduce | flops 131072 | bytes 786432 | tf_op jit(solution)/shard_map/psum | solution.py:53
  160.9 6.0 %fusion.6 = f32[2,32,2048]{2,1,0:T(8,128)S(1)} fusion(bf16[1,2048,2048]{2,1,0:T(8,128)(2,1)} %param.5, bf16[2,32,2048]{2,1,0:T(8,128)(2,1)S(1)} %all-reduce.7), kind=kOutput, calls=%fused_computation.7 | convolution fusion | flops 536870912 | bytes 9175040 | tf_op jit(solution)/shard_map/ekc,rc->ekr/dot_general | solution.py:29
  167.0 2.9 collective-permute-start.13
  169.9 11.5 %collective-permute-done.13 = f32[32,2048]{1,0:T(8,128)S(1)} collective-permute-done((f32[32,2048]{1,0:T(8,128)S(1)}, f32[32,2048]{1,0:T(8,128)S(1)}, u32[]{:S(2)}, u32[]{:S(2)}) %collective-permute-start.13) | collective-permute-done | bytes 262176 | tf_op jit(solution)/shard_map/ppermute | solution.py:12
  181.5 0.6 fusion.18
  182.2 1.2 collective-permute-done.15
  183.4 0.4 collective-permute-start.16
  183.8 3.5 %collective-permute-done.16 = f32[2,32,32]{1,2,0:T(8,128)S(1)} collective-permute-done((f32[2,32,32]{1,2,0:T(8,128)S(1)}, f32[2,32,32]{1,2,0:T(8,128)S(1)}, u32[]{:S(2)}, u32[]{:S(2)}) %collective-permute-start.16) | collective-permute-done | bytes 8224 | tf_op jit(solution)/shard_map/ppermute | solution.py:41
  187.4 5.9 %custom-call.16 = f32[2,32,32]{2,1,0:T(8,128)S(1)} custom-call(f32[2,32,32]{2,1,0:T(8,128)S(1)} %fusion.37), custom_call_target="Cholesky" | custom-call | tf_op jit(solution)/shard_map/jit(cholesky)/cholesky | solution.py:45
  193.5 4.9 %custom-call.17 = f32[2,1,32,32]{2,3,1,0:T(8,128)S(1)} custom-call(f32[2,1,32,32]{3,2,1,0:T(8,128)S(1)} %select_bitcast_fusion.1), custom_call_target="InvertDiagBlocksLowerTriangular" | custom-call | tf_op jit(solution)/shard_map/vmap(jit(_solve_triangular))/triangular_solve | solution.py:16
  198.4 0.7 convolution_convert_fusion.1
  199.0 5.0 %fusion.4 = f32[2,32,2048]{2,1,0:T(8,128)S(1)} fusion(bf16[2,32,2048]{2,1,0:T(8,128)(2,1)S(1)} %convolution_convert_fusion.1, bf16[1,2048,2048]{2,1,0:T(8,128)(2,1)} %param.5), kind=kOutput, calls=%fused_computation.5 | convolution fusion | flops 536870912 | bytes 9175040 | tf_op jit(solution)/shard_map/ekr,rc->ekc/dot_general | solution.py:48
  204.0 1.6 collective-permute-start.17
  205.7 0.4 collective-permute-start.18
  206.1 10.9 %collective-permute-done.17 = f32[32,2048]{1,0:T(8,128)S(1)} collective-permute-done((f32[32,2048]{1,0:T(8,128)S(1)}, f32[32,2048]{1,0:T(8,128)S(1)}, u32[]{:S(2)}, u32[]{:S(2)}) %collective-permute-start.17) | collective-permute-done | bytes 262176 | tf_op jit(solution)/shard_map/ppermute | solution.py:12
  217.1 15.9 %all-reduce.8 = bf16[2,32,2048]{2,1,0:T(8,128)(2,1)S(1)} all-reduce(f32[2,32,2048]{2,1,0:T(8,128)S(1)} %pad_maximum_fusion.5), channel_id=1, replica_groups=mesh['blk'=8,'shard'=4] {'shard'}, use_global_device_ids=true, to_apply=%region_4.7 | all-reduce | flops 131072 | bytes 786432 | tf_op jit(solution)/shard_map/psum | solution.py:53
  233.1 6.0 %fusion.2 = f32[2,32,2048]{2,1,0:T(8,128)S(1)} fusion(bf16[1,2048,2048]{2,1,0:T(8,128)(2,1)} %param.5, bf16[2,32,2048]{2,1,0:T(8,128)(2,1)S(1)} %all-reduce.8), kind=kOutput, calls=%fused_computation.3 | convolution fusion | flops 536870912 | bytes 9175040 | tf_op jit(solution)/shard_map/ekc,rc->ekr/dot_general | solution.py:29
  239.2 3.0 collective-permute-start.19
  242.1 11.4 %collective-permute-done.19 = f32[32,2048]{1,0:T(8,128)S(1)} collective-permute-done((f32[32,2048]{1,0:T(8,128)S(1)}, f32[32,2048]{1,0:T(8,128)S(1)}, u32[]{:S(2)}, u32[]{:S(2)}) %collective-permute-start.19) | collective-permute-done | bytes 262176 | tf_op jit(solution)/shard_map/ppermute | solution.py:12
  253.7 0.6 fusion.17
  254.3 1.2 collective-permute-done.21
  255.5 1.0 collective-permute-start.22
  256.5 2.9 collective-permute-done.22
  259.5 5.9 %custom-call.18 = f32[2,32,32]{2,1,0:T(8,128)S(1)} custom-call(f32[2,32,32]{2,1,0:T(8,128)S(1)} %fusion.35), custom_call_target="Cholesky" | custom-call | tf_op jit(solution)/shard_map/jit(cholesky)/cholesky | solution.py:45
  265.6 4.9 %custom-call.19 = f32[2,1,32,32]{2,3,1,0:T(8,128)S(1)} custom-call(f32[2,1,32,32]{3,2,1,0:T(8,128)S(1)} %select_bitcast_fusion), custom_call_target="InvertDiagBlocksLowerTriangular" | custom-call | tf_op jit(solution)/shard_map/vmap(jit(_solve_triangular))/triangular_solve | solution.py:16
  270.5 0.7 convolution_convert_fusion
  271.2 4.9 %fusion = f32[2,32,2048]{2,1,0:T(8,128)S(1)} fusion(bf16[2,32,2048]{2,1,0:T(8,128)(2,1)S(1)} %convolution_convert_fusion, bf16[1,2048,2048]{2,1,0:T(8,128)(2,1)} %param.5), kind=kOutput, calls=%fused_computation.1 | convolution fusion | flops 536870912 | bytes 9175040 | tf_op jit(solution)/shard_map/ekr,rc->ekc/dot_general | solution.py:48
  276.2 2.9 collective-permute-start.23
  279.1 10.7 %collective-permute-done.23 = f32[32,2048]{1,0:T(8,128)S(1)} collective-permute-done((f32[32,2048]{1,0:T(8,128)S(1)}, f32[32,2048]{1,0:T(8,128)S(1)}, u32[]{:S(2)}, u32[]{:S(2)}) %collective-permute-start.23) | collective-permute-done | bytes 262176 | tf_op jit(solution)/shard_map/ppermute | solution.py:12
  289.9 0.8 pad_maximum_fusion.7
  290.8 33.4 %all-reduce.5.cloned.1.call-done = f32[2,32,2048]{2,1,0:T(8,128)} async-done(((f32[2,32,2048]{2,1,0:T(8,128)}), f32[2,32,2048]{2,1,0:T(8,128)}) %all-reduce.5.cloned.1.call-update) | async-done | bytes 524304 | tf_op jit(solution)/shard_map/psum | solution.py:53
  324.1 1.1 convert_element_type.47
  325.2 6.9 %fusion.16 = bf16[1,2048,2048]{2,1,0:T(8,128)(2,1)} fusion(bf16[1,2048,2048]{2,1,0:T(8,128)(2,1)} %param.5, bf16[32,2048]{1,0:T(8,128)(2,1)S(1)} %get-tuple-element.39, bf16[32,2048]{1,0:T(8,128)(2,1)S(1)} %get-tuple-element.38, bf16[32,2048]{1,0:T(8,128)(2,1)S(1)} %get-tuple-element.37, bf16[32,2048]{1,0:T(8,128)(2,1)S(1)} %get-tuple-element.36), kind=kOutput, calls=%fused_computation.17 | convolution fusion | flops 554696704 | bytes 17301504 | tf_op jit(solution)/shard_map/jr,jc->rc/dot_general | solution.py:60
  332.1 1.5 constant_dynamic-slice_fusion
  (73 shorter events, 3.0 us)
Async XLA Ops:
  7.2 317.0 %all-reduce.5.cloned.1.call-start = ((), (), s32[]{:S(2)}) async-start(), calls=%async_computation | async-start | bytes 1048576 | tf_op jit(solution)/shard_map/psum | solution.py:53
  8.2 9.6 %collective-permute-start = (bf16[32,2048]{1,0:T(8,128)(2,1)S(1)}, bf16[32,2048]{1,0:T(8,128)(2,1)S(1)}, u32[]{:S(2)}, u32[]{:S(2)}) collective-permute-start(bf16[32,2048]{1,0:T(8,128)(2,1)S(1)} %convert_bitcast_fusion), channel_id=1, source_target_pairs={{0,4},{4,8},{8,12},{12,16},{16,20},{20,24},{24,28},{28,0},{1,5},{5... | collective-permute-start | bytes 393224 | tf_op jit(solution)/shard_map/ppermute | solution.py:12
  23.8 13.2 %collective-permute-start.1 = (f32[32,2048]{1,0:T(8,128)S(1)}, f32[32,2048]{1,0:T(8,128)S(1)}, u32[]{:S(2)}, u32[]{:S(2)}) collective-permute-start(f32[32,2048]{1,0:T(8,128)S(1)} %get-tuple-element.34), channel_id=1, source_target_pairs={{0,28},{4,0},{8,4},{12,8},{16,12},{20,16},{24,20},{28,24},{1,29},{... | collective-permute-start | bytes 786440 | tf_op jit(solution)/shard_map/ppermute | solution.py:12
  25.6 11.4 %collective-permute-start.2 = (f32[32,2048]{1,0:T(8,128)S(1)}, f32[32,2048]{1,0:T(8,128)S(1)}, u32[]{:S(2)}, u32[]{:S(2)}) collective-permute-start(f32[32,2048]{1,0:T(8,128)S(1)} %get-tuple-element.35), channel_id=1, source_target_pairs={{0,4},{4,8},{8,12},{12,16},{16,20},{20,24},{24,28},{28,0},{1,5},{5... | collective-permute-start | bytes 786440 | tf_op jit(solution)/shard_map/ppermute | solution.py:12
  37.6 1.3 collective-permute-start.3
  38.9 3.9 %collective-permute-start.4 = (f32[2,32,32]{1,2,0:T(8,128)S(1)}, f32[2,32,32]{1,2,0:T(8,128)S(1)}, u32[]{:S(2)}, u32[]{:S(2)}) collective-permute-start(f32[2,32,32]{1,2,0:T(8,128)S(1)} %add.47), channel_id=1, source_target_pairs={{0,2},{1,3},{2,0},{3,1},{4,6},{5,7},{6,4},{7,5},{8,10},{9,11},{10,... | collective-permute-start | bytes 24584 | tf_op jit(solution)/shard_map/ppermute | solution.py:41
  59.6 12.9 %collective-permute-start.5 = (f32[32,2048]{1,0:T(8,128)S(1)}, f32[32,2048]{1,0:T(8,128)S(1)}, u32[]{:S(2)}, u32[]{:S(2)}) collective-permute-start(f32[32,2048]{1,0:T(8,128)S(1)} %get-tuple-element.30), channel_id=1, source_target_pairs={{0,28},{4,0},{8,4},{12,8},{16,12},{20,16},{24,20},{28,24},{1,29},{... | collective-permute-start | bytes 786440 | tf_op jit(solution)/shard_map/ppermute | solution.py:12
  62.2 10.3 %collective-permute-start.6 = (f32[32,2048]{1,0:T(8,128)S(1)}, f32[32,2048]{1,0:T(8,128)S(1)}, u32[]{:S(2)}, u32[]{:S(2)}) collective-permute-start(f32[32,2048]{1,0:T(8,128)S(1)} %get-tuple-element.31), channel_id=1, source_target_pairs={{0,4},{4,8},{8,12},{12,16},{16,20},{20,24},{24,28},{28,0},{1,5},{5... | collective-permute-start | bytes 786440 | tf_op jit(solution)/shard_map/ppermute | solution.py:12
  94.9 14.0 %collective-permute-start.7 = (f32[32,2048]{1,0:T(8,128)S(1)}, f32[32,2048]{1,0:T(8,128)S(1)}, u32[]{:S(2)}, u32[]{:S(2)}) collective-permute-start(f32[32,2048]{1,0:T(8,128)S(1)} %get-tuple-element.26), channel_id=1, source_target_pairs={{0,28},{4,0},{8,4},{12,8},{16,12},{20,16},{24,20},{28,24},{1,29},{... | collective-permute-start | bytes 786440 | tf_op jit(solution)/shard_map/ppermute | solution.py:12
  97.7 11.2 %collective-permute-start.8 = (f32[32,2048]{1,0:T(8,128)S(1)}, f32[32,2048]{1,0:T(8,128)S(1)}, u32[]{:S(2)}, u32[]{:S(2)}) collective-permute-start(f32[32,2048]{1,0:T(8,128)S(1)} %get-tuple-element.27), channel_id=1, source_target_pairs={{0,4},{4,8},{8,12},{12,16},{16,20},{20,24},{24,28},{28,0},{1,5},{5... | collective-permute-start | bytes 786440 | tf_op jit(solution)/shard_map/ppermute | solution.py:12
  109.5 1.3 collective-permute-start.9
  110.8 3.9 %collective-permute-start.10 = (f32[2,32,32]{1,2,0:T(8,128)S(1)}, f32[2,32,32]{1,2,0:T(8,128)S(1)}, u32[]{:S(2)}, u32[]{:S(2)}) collective-permute-start(f32[2,32,32]{1,2,0:T(8,128)S(1)} %add.49), channel_id=1, source_target_pairs={{0,2},{1,3},{2,0},{3,1},{4,6},{5,7},{6,4},{7,5},{8,10},{9,11},{10,... | collective-permute-start | bytes 24584 | tf_op jit(solution)/shard_map/ppermute | solution.py:41
  131.5 12.9 %collective-permute-start.11 = (f32[32,2048]{1,0:T(8,128)S(1)}, f32[32,2048]{1,0:T(8,128)S(1)}, u32[]{:S(2)}, u32[]{:S(2)}) collective-permute-start(f32[32,2048]{1,0:T(8,128)S(1)} %get-tuple-element.22), channel_id=1, source_target_pairs={{0,28},{4,0},{8,4},{12,8},{16,12},{20,16},{24,20},{28,24},{1,29},{... | collective-permute-start | bytes 786440 | tf_op jit(solution)/shard_map/ppermute | solution.py:12
  134.3 10.1 %collective-permute-start.12 = (f32[32,2048]{1,0:T(8,128)S(1)}, f32[32,2048]{1,0:T(8,128)S(1)}, u32[]{:S(2)}, u32[]{:S(2)}) collective-permute-start(f32[32,2048]{1,0:T(8,128)S(1)} %get-tuple-element.23), channel_id=1, source_target_pairs={{0,4},{4,8},{8,12},{12,16},{16,20},{20,24},{24,28},{28,0},{1,5},{5... | collective-permute-start | bytes 786440 | tf_op jit(solution)/shard_map/ppermute | solution.py:12
  167.0 14.4 %collective-permute-start.13 = (f32[32,2048]{1,0:T(8,128)S(1)}, f32[32,2048]{1,0:T(8,128)S(1)}, u32[]{:S(2)}, u32[]{:S(2)}) collective-permute-start(f32[32,2048]{1,0:T(8,128)S(1)} %get-tuple-element.18), channel_id=1, source_target_pairs={{0,28},{4,0},{8,4},{12,8},{16,12},{20,16},{24,20},{28,24},{1,29},{... | collective-permute-start | bytes 786440 | tf_op jit(solution)/shard_map/ppermute | solution.py:12
  169.9 11.5 %collective-permute-start.14 = (f32[32,2048]{1,0:T(8,128)S(1)}, f32[32,2048]{1,0:T(8,128)S(1)}, u32[]{:S(2)}, u32[]{:S(2)}) collective-permute-start(f32[32,2048]{1,0:T(8,128)S(1)} %get-tuple-element.19), channel_id=1, source_target_pairs={{0,4},{4,8},{8,12},{12,16},{16,20},{20,24},{24,28},{28,0},{1,5},{5... | collective-permute-start | bytes 786440 | tf_op jit(solution)/shard_map/ppermute | solution.py:12
  182.1 1.3 collective-permute-start.15
  183.4 3.9 %collective-permute-start.16 = (f32[2,32,32]{1,2,0:T(8,128)S(1)}, f32[2,32,32]{1,2,0:T(8,128)S(1)}, u32[]{:S(2)}, u32[]{:S(2)}) collective-permute-start(f32[2,32,32]{1,2,0:T(8,128)S(1)} %add.51), channel_id=1, source_target_pairs={{0,2},{1,3},{2,0},{3,1},{4,6},{5,7},{6,4},{7,5},{8,10},{9,11},{10,... | collective-permute-start | bytes 24584 | tf_op jit(solution)/shard_map/ppermute | solution.py:41
  204.0 13.0 %collective-permute-start.17 = (f32[32,2048]{1,0:T(8,128)S(1)}, f32[32,2048]{1,0:T(8,128)S(1)}, u32[]{:S(2)}, u32[]{:S(2)}) collective-permute-start(f32[32,2048]{1,0:T(8,128)S(1)} %get-tuple-element.14), channel_id=1, source_target_pairs={{0,28},{4,0},{8,4},{12,8},{16,12},{20,16},{24,20},{28,24},{1,29},{... | collective-permute-start | bytes 786440 | tf_op jit(solution)/shard_map/ppermute | solution.py:12
  205.7 11.3 %collective-permute-start.18 = (f32[32,2048]{1,0:T(8,128)S(1)}, f32[32,2048]{1,0:T(8,128)S(1)}, u32[]{:S(2)}, u32[]{:S(2)}) collective-permute-start(f32[32,2048]{1,0:T(8,128)S(1)} %get-tuple-element.15), channel_id=1, source_target_pairs={{0,4},{4,8},{8,12},{12,16},{16,20},{20,24},{24,28},{28,0},{1,5},{5... | collective-permute-start | bytes 786440 | tf_op jit(solution)/shard_map/ppermute | solution.py:12
  239.2 14.4 %collective-permute-start.19 = (f32[32,2048]{1,0:T(8,128)S(1)}, f32[32,2048]{1,0:T(8,128)S(1)}, u32[]{:S(2)}, u32[]{:S(2)}) collective-permute-start(f32[32,2048]{1,0:T(8,128)S(1)} %get-tuple-element.10), channel_id=1, source_target_pairs={{0,28},{4,0},{8,4},{12,8},{16,12},{20,16},{24,20},{28,24},{1,29},{... | collective-permute-start | bytes 786440 | tf_op jit(solution)/shard_map/ppermute | solution.py:12
  242.1 11.5 %collective-permute-start.20 = (f32[32,2048]{1,0:T(8,128)S(1)}, f32[32,2048]{1,0:T(8,128)S(1)}, u32[]{:S(2)}, u32[]{:S(2)}) collective-permute-start(f32[32,2048]{1,0:T(8,128)S(1)} %get-tuple-element.11), channel_id=1, source_target_pairs={{0,4},{4,8},{8,12},{12,16},{16,20},{20,24},{24,28},{28,0},{1,5},{5... | collective-permute-start | bytes 786440 | tf_op jit(solution)/shard_map/ppermute | solution.py:12
  254.2 1.3 collective-permute-start.21
  255.5 3.9 %collective-permute-start.22 = (f32[2,32,32]{1,2,0:T(8,128)S(1)}, f32[2,32,32]{1,2,0:T(8,128)S(1)}, u32[]{:S(2)}, u32[]{:S(2)}) collective-permute-start(f32[2,32,32]{1,2,0:T(8,128)S(1)} %add.53), channel_id=1, source_target_pairs={{0,2},{1,3},{2,0},{3,1},{4,6},{5,7},{6,4},{7,5},{8,10},{9,11},{10,... | collective-permute-start | bytes 24584 | tf_op jit(solution)/shard_map/ppermute | solution.py:41
  276.2 13.6 %collective-permute-start.23 = (f32[32,2048]{1,0:T(8,128)S(1)}, f32[32,2048]{1,0:T(8,128)S(1)}, u32[]{:S(2)}, u32[]{:S(2)}) collective-permute-start(f32[32,2048]{1,0:T(8,128)S(1)} %get-tuple-element.6), channel_id=1, source_target_pairs={{0,28},{4,0},{8,4},{12,8},{16,12},{20,16},{24,20},{28,24},{1,29},{... | collective-permute-start | bytes 786440 | tf_op jit(solution)/shard_map/ppermute | solution.py:12
  279.1 10.7 %collective-permute-start.24 = (f32[32,2048]{1,0:T(8,128)S(1)}, f32[32,2048]{1,0:T(8,128)S(1)}, u32[]{:S(2)}, u32[]{:S(2)}) collective-permute-start(f32[32,2048]{1,0:T(8,128)S(1)} %get-tuple-element.7), channel_id=1, source_target_pairs={{0,4},{4,8},{8,12},{12,16},{16,20},{20,24},{24,28},{28,0},{1,5},{5... | collective-permute-start | bytes 786440 | tf_op jit(solution)/shard_map/ppermute | solution.py:12
Sparse Core Ops, SparseCore 0:
  290.9 33.2 all-reduce.4
